TPU v7x, 512 devices: a whole 4x8x8 slice. The times are simulated.
512 devices in a mesh: segment: 8 (over x, core), dev: 64 (over z, y).
Axes of the slice: x: 4, y: 8, z: 8, core: 2. Of those that a mesh axis runs over, the one named last changes fastest.
Arguments:
- queries: bfloat16 [512, 8192], P(('segment', 'dev')), may hold values from -64 to 64
- page_ids: int32 [512, 4, 32], P(('segment', 'dev')), may hold values from 0 to 1023, as said below
- key_pages: bfloat16 [8192, 64, 128], P(('segment', 'dev')), may hold values from -6 to 6
- value_pages: bfloat16 [8192, 64, 128], P(('segment', 'dev')), may hold values from -6 to 6
- out_weight: bfloat16 [65536, 16384], P(('segment', 'dev')), may hold values from -0.1875 to 0.1875
Outputs:
- block_out: bfloat16 [512, 16384], P(('segment', 'dev'))
Inputs may be any that keep to these rules, and one draw needn't show every extreme that they name: `page_ids`: within the rows of one device (aligned blocks of 1 row), at most 4 of the entries name pages of one device (id // 16); in every section one such device, the same for all of its row blocks, is named exactly 4 times from each block. The 32 ids of one row and key head are distinct.
All inputs are finite; a program needn't handle non-finite values.
Results may differ from a plain program's by a relative error of at most 0.006.
Values may be sent and summed in bfloat16 or wider, within the bound.
No kernel may reach another device: no remote copies, remote signals or barrier semaphores. Data moves between devices by JAX's collectives and lax.ppermute only.
A program may use at most 64 MiB of HBM per device.

v0:
```python
import math
import jax
import jax.numpy as jnp
from jax import lax
from jax.sharding import PartitionSpec as P


def from_behind(value, axis, steps):
    count = lax.axis_size(axis)
    pairs = [(source, (source + steps) % count) for source in range(count)]
    return lax.ppermute(value, axis, pairs)


def request_layout(page_ids, pool_size, devices, capacity):
    owner_ids = (page_ids // pool_size).reshape(-1)
    slot_ids = (page_ids % pool_size).reshape(-1)
    onehot = (owner_ids[:, None] == jnp.arange(devices, dtype=jnp.int32)[None, :]).astype(jnp.int32)
    before = jnp.cumsum(onehot, axis=0) - onehot
    rank_ids = jnp.sum(before * onehot, axis=1)
    target = owner_ids * capacity + rank_ids
    slot_table = jnp.zeros((devices * capacity,), jnp.int32).at[target].set(slot_ids)
    return (target, slot_table.reshape(devices, capacity))


def page_partials(query_part, key_part, value_part, score_scale):
    scores = (
        jnp.einsum("...gd,...td->...gt", query_part, key_part, preferred_element_type=jnp.float32)
        * score_scale
    )
    page_max = jnp.max(scores, axis=-1)
    weights = jnp.exp(scores - page_max[..., None]).astype(jnp.bfloat16)
    weight_sum = jnp.sum(weights.astype(jnp.float32), axis=-1)
    partial_value = jnp.einsum(
        "...gt,...td->...gd", weights, value_part, preferred_element_type=jnp.float32
    )
    return (partial_value, page_max, weight_sum)


def local(queries, page_ids, key_pages, value_pages, out_weight):
    devices = lax.axis_size("dev")
    row_count = queries.shape[0]
    kv_heads = page_ids.shape[1]
    chosen = page_ids.shape[2]
    pool_size = key_pages.shape[0]
    page_tokens = key_pages.shape[1]
    head_dim = key_pages.shape[2]
    group_size = queries.shape[1] // (kv_heads * head_dim)
    capacity = 2 * row_count * kv_heads * chosen // devices
    score_scale = 1.0 / math.sqrt(head_dim)
    target, slot_table = request_layout(page_ids, pool_size, devices, capacity)
    grouped = queries.reshape(row_count, kv_heads, 1, group_size, head_dim)
    per_request = jnp.broadcast_to(grouped, (row_count, kv_heads, chosen, group_size, head_dim))
    per_request = per_request.reshape(-1, group_size, head_dim)
    asked_slots = lax.all_to_all(slot_table, "dev", split_axis=0, concat_axis=0, tiled=True)
    fetched_keys, fetched_values = (
        lax.all_to_all(key_pages[asked_slots], "dev", split_axis=0, concat_axis=0, tiled=True),
        lax.all_to_all(value_pages[asked_slots], "dev", split_axis=0, concat_axis=0, tiled=True),
    )
    request_keys = fetched_keys.reshape(devices * capacity, page_tokens, head_dim)[target]
    request_values = fetched_values.reshape(devices * capacity, page_tokens, head_dim)[target]
    partial_value, page_max, weight_sum = page_partials(
        per_request, request_keys, request_values, score_scale
    )
    request_shape = (row_count, kv_heads, chosen, group_size)
    page_max = page_max.reshape(request_shape)
    weight_sum = weight_sum.reshape(request_shape)
    partial_value = partial_value.reshape(request_shape + (head_dim,))
    highest = jnp.max(page_max, axis=2, keepdims=True)
    factor = jnp.exp(page_max - highest)
    numerator = jnp.sum(factor[..., None] * partial_value, axis=2)
    denominator = jnp.sum(factor * weight_sum, axis=2)
    attended = (numerator / denominator[..., None]).astype(jnp.bfloat16)
    attended = attended.reshape(row_count, devices, -1)
    by_heads = lax.all_to_all(attended, "dev", split_axis=1, concat_axis=0, tiled=True)
    by_heads = by_heads.reshape(row_count * devices, -1)
    projected = lax.psum_scatter(
        jnp.dot(by_heads, out_weight, preferred_element_type=jnp.float32),
        "dev",
        scatter_dimension=0,
        tiled=True,
    ).astype(jnp.bfloat16)
    return from_behind(projected, "segment", 1)


def solution(mesh):
    placed = (
        P(("segment", "dev"), None),
        P(("segment", "dev"), None, None),
        P(("segment", "dev"), None, None),
        P(("segment", "dev"), None, None),
        P(("segment", "dev"), None),
    )
    return jax.shard_map(
        local, mesh=mesh, in_specs=placed, out_specs=P(("segment", "dev"), None), check_vma=False
    )
```

profile of v0, /device:TPU:1, one launch (start us, length us, event | category | flops | bytes accessed | tf_op | source)
XLA Modules:
  0.0 664.7 jit_solution(18260836763687210046)
XLA Ops:
  0.0 0.7 broadcast_multiply_fusion
  1.4 1.0 scatter_custom_fusion
  2.5 27.8 %all_to_all.31 = s32[64,1,4]{2,1,0:T(1,128)S(1)} all-to-all(s32[64,1,4]{2,1,0:T(1,128)S(1)} %bitcast.42), channel_id=1, replica_groups=mesh['segment'=8,'dev'=64] {'dev'}, dimensions={0} | all-to-all | bytes 2048 | tf_op jit(solution)/shard_map/all_to_all | solution.py:54
  30.5 3.1 gather_fusion
  33.5 5.8 all-to-all-start.1
  39.3 3.1 gather_fusion.2
  42.4 100.4 %all-to-all-done.1 = bf16[64,4,64,128]{3,2,1,0:T(8,128)(2,1)} async-done(((bf16[64,4,64,128]{3,2,1,0:T(8,128)(2,1)}), bf16[64,4,64,128]{3,2,1,0:T(8,128)(2,1)}, u32[]{:S(2)}, u32[]{:S(2)}) %all-to-all-start.1) | async-done | bytes 4194336 | tf_op jit(solution)/shard_map/all_to_all | solution.py:56
  142.8 37.4 %all-to-all-start.2 = ((bf16[64,4,64,128]{3,2,1,0:T(8,128)(2,1)}), bf16[64,4,64,128]{3,2,1,0:T(8,128)(2,1)}, u32[]{:S(2)}, u32[]{:S(2)}) async-start(bf16[64,4,64,128]{3,2,1,0:T(8,128)(2,1)} %bitcast.35), calls=%async_computation.2 | async-start | bytes 8388608 | tf_op jit(solution)/shard_map/all_to_all | solution.py:57
  180.3 3.1 gather_fusion.1
  183.6 1.3 fusion.11
  184.9 0.7 convert_reduce_fusion
  185.7 95.0 %all-to-all-done.2 = bf16[64,4,64,128]{3,2,1,0:T(8,128)(2,1)} async-done(((bf16[64,4,64,128]{3,2,1,0:T(8,128)(2,1)}), bf16[64,4,64,128]{3,2,1,0:T(8,128)(2,1)}, u32[]{:S(2)}, u32[]{:S(2)}) %all-to-all-start.2) | async-done | bytes 4194336 | tf_op jit(solution)/shard_map/all_to_all | solution.py:57
  280.7 3.1 gather_fusion.3
  283.9 0.7 fusion.1
  285.0 0.8 divide_convert_fusion
  285.7 29.6 %all-to-all-start.3 = ((bf16[1,64,128]{2,0,1:T(2,128)(2,1)}), bf16[1,64,128]{2,0,1:T(2,128)(2,1)S(1)}, u32[]{:S(2)}, u32[]{:S(2)}) async-start(bf16[1,64,128]{2,0,1:T(2,128)(2,1)} %divide_convert_fusion), calls=%async_computation.3 | async-start | bytes 65536 | tf_op jit(solution)/shard_map/all_to_all | solution.py:74
  315.3 1.3 dynamic-slice
  316.6 9.5 %all-to-all-done.3 = bf16[1,64,128]{2,0,1:T(2,128)(2,1)S(1)} async-done(((bf16[1,64,128]{2,0,1:T(2,128)(2,1)}), bf16[1,64,128]{2,0,1:T(2,128)(2,1)S(1)}, u32[]{:S(2)}, u32[]{:S(2)}) %all-to-all-start.3) | async-done | bytes 16416 | tf_op jit(solution)/shard_map/all_to_all | solution.py:74
  326.1 4.8 fusion.4
  330.9 272.3 %all-reduce.2 = bf16[64,16384]{1,0:T(8,128)(2,1)S(1)} all-reduce(f32[64,16384]{1,0:T(8,128)} %fusion.4), channel_id=2, replica_groups=mesh['segment'=8,'dev'=64] {'dev'}, use_global_device_ids=true, to_apply=%region_8.9.clone | all-reduce | flops 1048576 | bytes 6291456
  603.2 0.7 dynamic-slice_convert_fusion
  603.9 58.8 %collective-permute-start = (bf16[1,16384]{1,0:T(2,128)(2,1)S(1)}, bf16[1,16384]{1,0:T(2,128)(2,1)S(1)}, u32[]{:S(2)}, u32[]{:S(2)}) collective-permute-start(bf16[1,16384]{1,0:T(2,128)(2,1)S(1)} %dynamic-slice_convert_fusion), channel_id=1, source_target_pairs={{0,64},{64,128},{128,192},{192,256},{256,320},{320,384},{384,448},... | collective-permute-start | bytes 98312 | tf_op jit(solution)/shard_map/ppermute | solution.py:11
  662.7 1.3 collective-permute-done
  664.1 0.6 copy.16
  (25 shorter events, 1.6 us)
Async XLA Ops:
  0.0 30.4 %copy-start = (bf16[16,64,128]{2,1,0:T(8,128)(2,1)S(1)}, bf16[16,64,128]{2,1,0:T(8,128)(2,1)}, u32[]{:S(2)}) copy-start(bf16[16,64,128]{2,1,0:T(8,128)(2,1)} %param.7) | copy-start | bytes 786436
  33.5 5.8 copy-start.1
  33.5 109.3 %all-to-all-start.1 = ((bf16[64,4,64,128]{3,2,1,0:T(8,128)(2,1)}), bf16[64,4,64,128]{3,2,1,0:T(8,128)(2,1)}, u32[]{:S(2)}, u32[]{:S(2)}) async-start(bf16[64,4,64,128]{3,2,1,0:T(8,128)(2,1)} %bitcast.36), calls=%async_computation.1 | async-start | bytes 8388608 | tf_op jit(solution)/shard_map/all_to_all | solution.py:56
  142.8 37.4 %copy-start.2 = (bf16[1,8192]{1,0:T(2,128)(2,1)S(1)}, bf16[1,8192]{1,0:T(2,128)(2,1)}, u32[]{:S(2)}) copy-start(bf16[1,8192]{1,0:T(2,128)(2,1)} %param.5) | copy-start | bytes 49156
  142.8 137.9 %all-to-all-start.2 = ((bf16[64,4,64,128]{3,2,1,0:T(8,128)(2,1)}), bf16[64,4,64,128]{3,2,1,0:T(8,128)(2,1)}, u32[]{:S(2)}, u32[]{:S(2)}) async-start(bf16[64,4,64,128]{3,2,1,0:T(8,128)(2,1)} %bitcast.35), calls=%async_computation.2 | async-start | bytes 8388608 | tf_op jit(solution)/shard_map/all_to_all | solution.py:57
  285.7 40.4 %all-to-all-start.3 = ((bf16[1,64,128]{2,0,1:T(2,128)(2,1)}), bf16[1,64,128]{2,0,1:T(2,128)(2,1)S(1)}, u32[]{:S(2)}, u32[]{:S(2)}) async-start(bf16[1,64,128]{2,0,1:T(2,128)(2,1)} %divide_convert_fusion), calls=%async_computation.3 | async-start | bytes 65536 | tf_op jit(solution)/shard_map/all_to_all | solution.py:74
  603.9 60.1 %collective-permute-start = (bf16[1,16384]{1,0:T(2,128)(2,1)S(1)}, bf16[1,16384]{1,0:T(2,128)(2,1)S(1)}, u32[]{:S(2)}, u32[]{:S(2)}) collective-permute-start(bf16[1,16384]{1,0:T(2,128)(2,1)S(1)} %dynamic-slice_convert_fusion), channel_id=1, source_target_pairs={{0,64},{64,128},{128,192},{192,256},{256,320},{320,384},{384,448},... | collective-permute-start | bytes 98312 | tf_op jit(solution)/shard_map/ppermute | solution.py:11
where the time goes:
time: 665 us
  blocking collectives  300 us (45%)
  waiting for transfers between devices  206 us (31%)
  starting transfers between devices  132 us (20%)
  local copies, waits for them, and re-layouts  16.6 us (2%)
  matrix products  6.83 us (1%)
    unnamed x1, blocking collectives  272 us
    all_to_all x1, waiting for transfers between devices, local(): lax.all_to_all(key_pages[asked_slots], 'dev', split_axis=0, concat_axis=0...  100 us
    all_to_all x1, waiting for transfers between devices, local(): lax.all_to_all(value_pages[asked_slots], 'dev', split_axis=0, concat_axis...  95 us
    ppermute x1, starting transfers between devices, from_behind(): return lax.ppermute(value, axis, pairs)  58.8 us
    all_to_all x1, starting transfers between devices, local(): lax.all_to_all(value_pages[asked_slots], 'dev', split_axis=0, concat_axis...  37.4 us
    all_to_all x1, starting transfers between devices, local(): lax.all_to_all(attended, 'dev', split_axis=1, concat_axis=0, tiled=True)  29.6 us
    all_to_all x1, blocking collectives, local(): lax.all_to_all(slot_table, 'dev', split_axis=0, concat_axis=0, tiled=True)  27.8 us
  transfers between devices with their start and end apart: 4, of which 4 were waited for; matrix products, arithmetic and copies ran while one was open for 1% of the time, Pallas kernels for 0%

commit v1 on v0

--- a/solution.py
+++ b/solution.py
@@ -71,7 +71,10 @@
     denominator = jnp.sum(factor * weight_sum, axis=2)
     attended = (numerator / denominator[..., None]).astype(jnp.bfloat16)
     attended = attended.reshape(row_count, devices, -1)
-    by_heads = lax.all_to_all(attended, "dev", split_axis=1, concat_axis=0, tiled=True)
+    by_heads = jnp.concatenate(
+        lax.all_to_all(jnp.stack(jnp.split(attended, lax.axis_size("dev"), axis=1)), "dev", 0, 0),
+        axis=0,
+    )
     by_heads = by_heads.reshape(row_count * devices, -1)
     projected = lax.psum_scatter(
         jnp.dot(by_heads, out_weight, preferred_element_type=jnp.float32),

time: 665 us -> 701 us (1.054)
  local copies, waits for them, and re-layouts: 16.6 us -> 50.7 us
    unnamed x8 -> x73, local copies, waits for them, and re-layouts: 1.92 us -> 34.3 us
where the time goes in v1:
time: 701 us; the launch traced here: 700 us
  blocking collectives  301 us (43%)
  waiting for transfers between devices  208 us (30%)
  starting transfers between devices  131 us (19%)
  local copies, waits for them, and re-layouts  50.7 us (7%)
    unnamed x1, blocking collectives  273 us
    all_to_all x1, waiting for transfers between devices, local(): lax.all_to_all(key_pages[asked_slots], 'dev', split_axis=0, concat_axis=0...  100 us
    all_to_all x1, waiting for transfers between devices, local(): lax.all_to_all(value_pages[asked_slots], 'dev', split_axis=0, concat_axis...  97.3 us
    ppermute x1, starting transfers between devices, from_behind(): return lax.ppermute(value, axis, pairs)  58 us
    all_to_all x1, starting transfers between devices, local(): lax.all_to_all(value_pages[asked_slots], 'dev', split_axis=0, concat_axis...  37.4 us
    unnamed x73, local copies, waits for them, and re-layouts  34.3 us
    all_to_all x1, starting transfers between devices, local(): lax.all_to_all(jnp.stack(jnp.split(attended, lax.axis_size('dev'), axis=1...  29.6 us
    all_to_all x1, blocking collectives, local(): lax.all_to_all(slot_table, 'dev', split_axis=0, concat_axis=0, tiled=True)  27.8 us
  transfers between devices with their start and end apart: 4, of which 4 were waited for; matrix products, arithmetic and copies ran while one was open for 1% of the time, Pallas kernels for 0%

profile of v1, /device:TPU:1, one launch (start us, length us, event | category | flops | bytes accessed | tf_op | source)
XLA Modules:
  0.0 700.2 jit_solution(9664748103489251034)
XLA Ops:
  0.0 0.7 broadcast_multiply_fusion
  1.4 1.0 scatter_custom_fusion
  2.5 27.8 %all_to_all.27 = s32[64,1,4]{2,1,0:T(1,128)S(1)} all-to-all(s32[64,1,4]{2,1,0:T(1,128)S(1)} %bitcast.302), channel_id=1, replica_groups=mesh['segment'=8,'dev'=64] {'dev'}, dimensions={0} | all-to-all | bytes 2048 | tf_op jit(solution)/shard_map/all_to_all | solution.py:54
  30.5 3.1 gather_fusion
  33.5 5.8 all-to-all-start.1
  39.3 3.1 gather_fusion.2
  42.4 100.4 %all-to-all-done.1 = bf16[64,4,64,128]{3,2,1,0:T(8,128)(2,1)} async-done(((bf16[64,4,64,128]{3,2,1,0:T(8,128)(2,1)}), bf16[64,4,64,128]{3,2,1,0:T(8,128)(2,1)}, u32[]{:S(2)}, u32[]{:S(2)}) %all-to-all-start.1) | async-done | bytes 4194336 | tf_op jit(solution)/shard_map/all_to_all | solution.py:56
  142.8 37.4 %all-to-all-start.2 = ((bf16[64,4,64,128]{3,2,1,0:T(8,128)(2,1)}), bf16[64,4,64,128]{3,2,1,0:T(8,128)(2,1)}, u32[]{:S(2)}, u32[]{:S(2)}) async-start(bf16[64,4,64,128]{3,2,1,0:T(8,128)(2,1)} %bitcast.295), calls=%async_computation.2 | async-start | bytes 8388608 | tf_op jit(solution)/shard_map/all_to_all | solution.py:57
  180.3 3.1 gather_fusion.1
  183.5 97.3 %all-to-all-done.2 = bf16[64,4,64,128]{3,2,1,0:T(8,128)(2,1)} async-done(((bf16[64,4,64,128]{3,2,1,0:T(8,128)(2,1)}), bf16[64,4,64,128]{3,2,1,0:T(8,128)(2,1)}, u32[]{:S(2)}, u32[]{:S(2)}) %all-to-all-start.2) | async-done | bytes 4194336 | tf_op jit(solution)/shard_map/all_to_all | solution.py:57
  280.7 4.4 gather_fusion.3
  285.2 1.3 fusion.12
  286.5 0.7 convert_reduce_fusion
  287.2 0.7 fusion.1
  289.0 0.5 constant_dynamic-update-slice_fusion.62
  321.4 29.6 %all-to-all-start.3 = ((bf16[64,1,1,128]{3,2,1,0:T(2,128)(2,1)}), bf16[64,1,1,128]{3,2,1,0:T(2,128)(2,1)S(1)}, u32[]{:S(2)}, u32[]{:S(2)}) async-start(bf16[64,1,1,128]{3,2,1,0:T(2,128)(2,1)} %constant_dynamic-update-slice_fusion), calls=%async_computation.3 | async-start | bytes 65536 | tf_op jit(solution)/shard_map/all_to_all | solution.py:75
  351.0 1.3 dynamic-slice
  352.3 9.5 %all-to-all-done.3 = bf16[64,1,1,128]{3,2,1,0:T(2,128)(2,1)S(1)} async-done(((bf16[64,1,1,128]{3,2,1,0:T(2,128)(2,1)}), bf16[64,1,1,128]{3,2,1,0:T(2,128)(2,1)S(1)}, u32[]{:S(2)}, u32[]{:S(2)}) %all-to-all-start.3) | async-done | bytes 16416 | tf_op jit(solution)/shard_map/all_to_all | solution.py:75
  361.8 4.8 fusion.5
  366.6 273.0 %all-reduce.2 = bf16[64,16384]{1,0:T(8,128)(2,1)S(1)} all-reduce(f32[64,16384]{1,0:T(8,128)} %fusion.5), channel_id=2, replica_groups=mesh['segment'=8,'dev'=64] {'dev'}, use_global_device_ids=true, to_apply=%region_8.9.clone | all-reduce | flops 1048576 | bytes 6291456
  639.6 0.7 dynamic-slice_convert_fusion
  640.3 58.0 %collective-permute-start = (bf16[1,16384]{1,0:T(2,128)(2,1)S(1)}, bf16[1,16384]{1,0:T(2,128)(2,1)S(1)}, u32[]{:S(2)}, u32[]{:S(2)}) collective-permute-start(bf16[1,16384]{1,0:T(2,128)(2,1)S(1)} %dynamic-slice_convert_fusion), channel_id=1, source_target_pairs={{0,64},{64,128},{128,192},{192,256},{256,320},{320,384},{384,448},... | collective-permute-start | bytes 98312 | tf_op jit(solution)/shard_map/ppermute | solution.py:11
  698.2 1.3 collective-permute-done
  699.6 0.6 copy.78
  (91 shorter events, 34.1 us)
Async XLA Ops:
  0.0 30.4 %copy-start = (bf16[16,64,128]{2,1,0:T(8,128)(2,1)S(1)}, bf16[16,64,128]{2,1,0:T(8,128)(2,1)}, u32[]{:S(2)}) copy-start(bf16[16,64,128]{2,1,0:T(8,128)(2,1)} %param.7) | copy-start | bytes 786436
  33.5 5.8 copy-start.1
  33.5 109.3 %all-to-all-start.1 = ((bf16[64,4,64,128]{3,2,1,0:T(8,128)(2,1)}), bf16[64,4,64,128]{3,2,1,0:T(8,128)(2,1)}, u32[]{:S(2)}, u32[]{:S(2)}) async-start(bf16[64,4,64,128]{3,2,1,0:T(8,128)(2,1)} %bitcast.296), calls=%async_computation.1 | async-start | bytes 8388608 | tf_op jit(solution)/shard_map/all_to_all | solution.py:56
  142.8 37.4 %copy-start.3 = (bf16[1,8192]{1,0:T(2,128)(2,1)S(1)}, bf16[1,8192]{1,0:T(2,128)(2,1)}, u32[]{:S(2)}) copy-start(bf16[1,8192]{1,0:T(2,128)(2,1)} %param.5) | copy-start | bytes 49156
  142.8 137.9 %all-to-all-start.2 = ((bf16[64,4,64,128]{3,2,1,0:T(8,128)(2,1)}), bf16[64,4,64,128]{3,2,1,0:T(8,128)(2,1)}, u32[]{:S(2)}, u32[]{:S(2)}) async-start(bf16[64,4,64,128]{3,2,1,0:T(8,128)(2,1)} %bitcast.295), calls=%async_computation.2 | async-start | bytes 8388608 | tf_op jit(solution)/shard_map/all_to_all | solution.py:57
  285.1 2.1 copy-start.2
  321.4 40.4 %all-to-all-start.3 = ((bf16[64,1,1,128]{3,2,1,0:T(2,128)(2,1)}), bf16[64,1,1,128]{3,2,1,0:T(2,128)(2,1)S(1)}, u32[]{:S(2)}, u32[]{:S(2)}) async-start(bf16[64,1,1,128]{3,2,1,0:T(2,128)(2,1)} %constant_dynamic-update-slice_fusion), calls=%async_computation.3 | async-start | bytes 65536 | tf_op jit(solution)/shard_map/all_to_all | solution.py:75
  640.3 59.3 %collective-permute-start = (bf16[1,16384]{1,0:T(2,128)(2,1)S(1)}, bf16[1,16384]{1,0:T(2,128)(2,1)S(1)}, u32[]{:S(2)}, u32[]{:S(2)}) collective-permute-start(bf16[1,16384]{1,0:T(2,128)(2,1)S(1)} %dynamic-slice_convert_fusion), channel_id=1, source_target_pairs={{0,64},{64,128},{128,192},{192,256},{256,320},{320,384},{384,448},... | collective-permute-start | bytes 98312 | tf_op jit(solution)/shard_map/ppermute | solution.py:11
